TPU v7x, 32 devices: a whole 2x2x4 slice. The times are simulated.
32 devices in a mesh: gx: 4 (over y, x), gy: 4 (over z), gz: 2 (over core).
Axes of the slice: x: 2, y: 2, z: 4, core: 2. Of those that a mesh axis runs over, the one named last changes fastest.
Arguments:
- displacement: bfloat16 [16, 4, 4, 12, 3, 32, 128], P('gx', 'gy', 'gz'), may hold values from -96 to 96
- dof_weight: bfloat16 [16, 4, 4, 12, 128], P('gx', 'gy', 'gz'), may hold values from 0.099609375 to 10
- coarse_matrix: float32 [16, 4, 4, 27, 36, 36], P('gx', 'gy', 'gz'), may hold values from -48 to 48, as said below
- block_inverse: float32 [16, 4, 4, 36, 36], P('gx', 'gy', 'gz'), may hold values from -12 to 12, as said below
Outputs:
- edge_average: float32 [16, 4, 4, 12, 3, 32], P('gx', 'gy', 'gz')
- coarse_solution: float32 [16, 4, 4, 36, 32], P('gx', 'gy', 'gz')
Inputs may be any that keep to these rules, and one draw needn't show every extreme that they name: coarse_matrix is the replicated form of one operator over edge unknowns: rows of the same edge seen from its four subdomains are equal, and each column of an edge is stored at exactly one of that edge's subdomains (zeros at the others). block_inverse[p] is block-diagonal in 3 x 3 blocks, each the inverse of the matching diagonal 3 x 3 block of coarse_matrix[p, 13].
All inputs are finite; a program needn't handle non-finite values.
Results may differ from a plain program's by a relative error of at most 0.0003.
Values sent between devices are 32-bit elements; how exact they have to be, the bound alone decides.
A program may use at most 64 MiB of HBM per device.

v0:
```python
import jax
import jax.numpy as jnp
from jax import lax
from jax.sharding import PartitionSpec as P

SWEEPS = 4
COARSE = 36


def passed_along(block, axis, distance):
    devices = range(lax.axis_size(axis))
    route = [((i - distance) % len(devices), i) for i in devices]
    return lax.ppermute(block, axis, route)


def with_halo(cells, sides, width):
    for axis, dim in sides:
        count = lax.axis_size(axis)
        head = lax.slice_in_dim(cells, 0, width, axis=dim)
        tail = lax.slice_in_dim(cells, cells.shape[dim] - width, cells.shape[dim], axis=dim)
        cells = jnp.concatenate(
            [
                lax.ppermute(tail, axis, [(i, (i + 1) % count) for i in range(count)]),
                cells,
                lax.ppermute(head, axis, [((i + 1) % count, i) for i in range(count)]),
            ],
            axis=dim,
        )
    return cells


def apply_matrix(padded, coarse_matrix, size_x, size_y, size_z):
    total = jnp.zeros((size_x, size_y, size_z) + padded.shape[3:], jnp.float32)
    for offset in range(27):
        start_x = offset // 9
        start_y = offset // 3 % 3
        start_z = offset % 3
        piece = padded[
            start_x : start_x + size_x, start_y : start_y + size_y, start_z : start_z + size_z
        ]
        total = total + jnp.einsum(
            "xyzij,xyzjr->xyzir",
            coarse_matrix[:, :, :, offset],
            piece,
            precision=lax.Precision.HIGHEST,
        )
    return total


def upper_border(array, dim):
    count = array.shape[dim]
    return lax.slice_in_dim(array, count - 1, count, axis=dim)


def lower_border(array, dim):
    return lax.slice_in_dim(array, 0, 1, axis=dim)


def from_below(array, received, dim):
    count = array.shape[dim]
    return jnp.concatenate([received, lax.slice_in_dim(array, 0, count - 1, axis=dim)], axis=dim)


def from_above(array, received, dim):
    count = array.shape[dim]
    return jnp.concatenate([lax.slice_in_dim(array, 1, count, axis=dim), received], axis=dim)


def body(displacement, dof_weight, coarse_matrix, block_inverse):
    size_x, size_y, size_z = (displacement.shape[0], displacement.shape[1], displacement.shape[2])
    numers = jnp.einsum(
        "xyzecrk,xyzek->xyzecr", displacement, dof_weight, preferred_element_type=jnp.float32
    )
    weights = jnp.sum(dof_weight.astype(jnp.float32), axis=-1)
    sources = [6, 7, 10, 11]
    targets = [4, 5, 8, 9]
    moving_numer = numers[:, :, :, sources]
    moving_weight = weights[:, :, :, sources]
    got_numer, got_weight = passed_along(
        (upper_border(moving_numer, 0), upper_border(moving_weight, 0)), "gx", 1
    )
    numers = numers.at[:, :, :, targets].add(from_below(moving_numer, got_numer, 0))
    weights = weights.at[:, :, :, targets].add(from_below(moving_weight, got_weight, 0))
    sources = [2, 3, 9]
    targets = [0, 1, 8]
    moving_numer = numers[:, :, :, sources]
    moving_weight = weights[:, :, :, sources]
    got_numer, got_weight = passed_along(
        (upper_border(moving_numer, 1), upper_border(moving_weight, 1)), "gy", 1
    )
    numers = numers.at[:, :, :, targets].add(from_below(moving_numer, got_numer, 1))
    weights = weights.at[:, :, :, targets].add(from_below(moving_weight, got_weight, 1))
    sources = [1, 5]
    targets = [0, 4]
    moving_numer = numers[:, :, :, sources]
    moving_weight = weights[:, :, :, sources]
    got_numer, got_weight = passed_along(
        (upper_border(moving_numer, 2), upper_border(moving_weight, 2)), "gz", 1
    )
    numers = numers.at[:, :, :, targets].add(from_below(moving_numer, got_numer, 2))
    weights = weights.at[:, :, :, targets].add(from_below(moving_weight, got_weight, 2))
    averages = numers / weights[..., None, None]
    moving = averages[:, :, :, [0, 4]]
    received = passed_along(lower_border(moving, 2), "gz", -1)
    averages = averages.at[:, :, :, [1, 5]].set(from_above(moving, received, 2))
    moving = averages[:, :, :, [0, 1, 8]]
    received = passed_along(lower_border(moving, 1), "gy", -1)
    averages = averages.at[:, :, :, [2, 3, 9]].set(from_above(moving, received, 1))
    moving = averages[:, :, :, [4, 5, 8, 9]]
    received = passed_along(lower_border(moving, 0), "gx", -1)
    averages = averages.at[:, :, :, [6, 7, 10, 11]].set(from_above(moving, received, 0))
    rhs_rows = averages.reshape(size_x, size_y, size_z, COARSE, averages.shape[-1])
    iterate = jnp.einsum(
        "xyzij,xyzjr->xyzir", block_inverse, rhs_rows, precision=lax.Precision.HIGHEST
    )
    for sweep in range(SWEEPS - 1):
        padded = with_halo(iterate, (("gx", 0), ("gy", 1), ("gz", 2)), 1)
        product = apply_matrix(padded, coarse_matrix, size_x, size_y, size_z)
        iterate = iterate + jnp.einsum(
            "xyzij,xyzjr->xyzir", block_inverse, rhs_rows - product, precision=lax.Precision.HIGHEST
        )
    return (averages, iterate)


def solution(mesh):
    placed = (
        P("gx", "gy", "gz", None, None, None, None),
        P("gx", "gy", "gz", None, None),
        P("gx", "gy", "gz", None, None, None),
        P("gx", "gy", "gz", None, None),
    )
    return jax.shard_map(
        body,
        mesh=mesh,
        in_specs=placed,
        out_specs=(P("gx", "gy", "gz", None, None, None), P("gx", "gy", "gz", None, None)),
        check_vma=False,
    )
```

profile of v0, /device:TPU:0, one launch (start us, length us, event | category | flops | bytes accessed | tf_op | source)
XLA Modules:
  0.0 141.5 jit_solution(5736743366843360824)
XLA Ops:
  3.3 2.9 %collective-permute-start.3 = (f32[1,1,2,4]{3,2,1,0:T(2,128)S(1)}, f32[1,1,2,4]{3,2,1,0:T(2,128)S(1)}, u32[]{:S(2)}, u32[]{:S(2)}) collective-permute-start(f32[1,1,2,4]{3,2,1,0:T(2,128)S(1)} %bitcast.691), channel_id=1, source_target_pairs={{24,0},{0,8},{8,16},{16,24},{25,1},{1,9},{9,17},{17,25},{26,2},{2,... | collective-permute-start | bytes 104 | tf_op jit(solution)/shard_map/ppermute | solution.py:13
  6.2 3.3 %fusion = f32[4,2,12,1,3,32]{5,3,4,2,1,0:T(1,128)S(1)} fusion(bf16[4,1,2,12,3,32,128]{6,5,4,3,2,1,0:T(8,128)(2,1)S(1)} %copy-done, bf16[4,2,12,128,1,1]{3,1,2,0,4,5:T(2,128)(2,1)} %bitcast.675), kind=kOutput, calls=%fused_computation.18 | convolution fusion | flops 2359296 | bytes 2420736 | tf_op jit(solution)/shard_map/xyzecrk,xyzek->xyzecr/dot_general | solution.py:71
  13.5 3.2 %fusion.94 = (f32[4,1,2,1,36,36]{5,2,4,3,1,0:T(2,128)}, f32[4,1,2,1,36,36]{5,2,4,3,1,0:T(2,128)}, f32[4,1,2,1,36,36]{5,2,4,3,1,0:T(2,128)S(1)}, f32[4,1,2,1,36,3...) fusion(f32[4,1,2,27,36,36]{5,2,4,3,1,0:T(2,128)} %param.24), kind=kLoop, calls=%fused_computation.322 | loop fusion | bytes 1575936 | tf_op jit(solution)/shard_map/slice | solution.py:43
  18.0 1.6 %collective-permute-start.4 = (f32[4,1,2,3]{0,2,3,1:T(2,128)S(1)}, f32[4,1,2,3]{0,2,3,1:T(2,128)S(1)}, u32[]{:S(2)}, u32[]{:S(2)}) collective-permute-start(f32[4,1,2,3]{0,2,3,1:T(2,128)S(1)} %bitcast.690), channel_id=1, source_target_pairs={{6,0},{0,2},{2,4},{4,6},{7,1},{1,3},{3,5},{5,7},{14,8},{8,10},{10,... | collective-permute-start | bytes 296 | tf_op jit(solution)/shard_map/ppermute | solution.py:13
  19.6 3.8 %collective-permute-done.4 = f32[4,1,2,3]{0,2,3,1:T(2,128)S(1)} collective-permute-done((f32[4,1,2,3]{0,2,3,1:T(2,128)S(1)}, f32[4,1,2,3]{0,2,3,1:T(2,128)S(1)}, u32[]{:S(2)}, u32[]{:S(2)}) %collective-permute-start.4) | collective-permute-done | bytes 128 | tf_op jit(solution)/shard_map/ppermute | solution.py:13
  24.7 2.0 %scatter_fusion = f32[4,2,12,3,32]{4,0,3,2,1:T(4,128)} fusion(f32[4,2,12,3,32]{4,0,3,2,1:T(4,128)} %bitcast.632, s32[4]{0:T(128)S(1)} %copy-done.16, f32[4,4,2,3,32]{4,1,3,2,0:T(4,128)S(1)} %maximum_bitcast_fusion), kind=kCustom, calls=%fused_computation.9 | custom fusion | flops 3072 | bytes 36880 | tf_op jit(solution)/shard_map/scatter-add | solution.py:82
  28.4 5.7 %collective-permute-done.1 = f32[4,1,2,3,3,32]{5,0,4,2,3,1:T(4,128)S(1)} collective-permute-done((f32[4,1,2,3,3,32]{5,0,4,2,3,1:T(4,128)S(1)}, f32[4,1,2,3,3,32]{5,0,4,2,3,1:T(4,128)S(1)}, u32[]{:S(2)}, u32[]{:S(2)}) %collective-permute-start.1) | collective-permute-done | bytes 9248 | tf_op jit(solution)/shard_map/ppermute | solution.py:13
  34.0 2.0 %scatter_fusion.1 = f32[4,2,12,3,32]{4,0,3,2,1:T(4,128)} fusion(f32[4,2,12,3,32]{4,0,3,2,1:T(4,128)} %scatter_fusion, s32[3]{0:T(128)S(1)} %copy-done.17, f32[3,4,2,3,32]{4,1,3,2,0:T(4,128)S(1)} %bitcast.680), kind=kCustom, calls=%fused_computation.10 | custom fusion | flops 2304 | bytes 27660 | tf_op jit(solution)/shard_map/scatter-add | solution.py:91
  38.7 1.9 %scatter_fusion.2 = f32[4,2,12,3,32]{4,0,3,2,1:T(4,128)} fusion(f32[4,2,12,3,32]{4,0,3,2,1:T(4,128)} %scatter_fusion.1, s32[2]{0:T(128)S(1)} %compare_select_fusion, f32[2,4,2,3,32]{4,1,3,2,0:T(4,128)S(1)} %maximum_bitcast_fusion.2), kind=kCustom, calls=%fused_computation.11 | custom fusion | flops 1536 | bytes 18440 | tf_op jit(solution)/shard_map/scatter-add | solution.py:100
  44.8 3.9 %collective-permute-done.7 = f32[4,1,2,3,3,32]{5,0,4,2,3,1:T(4,128)S(1)} collective-permute-done((f32[4,1,2,3,3,32]{5,0,4,2,3,1:T(4,128)S(1)}, f32[4,1,2,3,3,32]{5,0,4,2,3,1:T(4,128)S(1)}, u32[]{:S(2)}, u32[]{:S(2)}) %collective-permute-start.7) | collective-permute-done | bytes 9248 | tf_op jit(solution)/shard_map/ppermute | solution.py:13
  51.6 2.2 %collective-permute-done.8 = f32[1,1,2,4,3,32]{5,0,4,2,3,1:T(1,128)S(1)} collective-permute-done((f32[1,1,2,4,3,32]{5,0,4,2,3,1:T(1,128)S(1)}, f32[1,1,2,4,3,32]{5,0,4,2,3,1:T(1,128)S(1)}, u32[]{:S(2)}, u32[]{:S(2)}) %collective-permute-start.8) | collective-permute-done | bytes 3104 | tf_op jit(solution)/shard_map/ppermute | solution.py:13
  56.7 2.4 %collective-permute-start.10 = (f32[1,1,2,36,32]{3,4,2,1,0:T(8,128)S(1)}, f32[1,1,2,36,32]{3,4,2,1,0:T(8,128)S(1)}, u32[]{:S(2)}, u32[]{:S(2)}) collective-permute-start(f32[1,1,2,36,32]{3,4,2,1,0:T(8,128)S(1)} %get-tuple-element.54), channel_id=1, source_target_pairs={{8,0},{16,8},{24,16},{0,24},{9,1},{17,9},{25,17},{1,25},{10,2},{18... | collective-permute-start | bytes 27656 | tf_op jit(solution)/shard_map/ppermute | solution.py:25
  61.1 2.9 %collective-permute-done.9 = f32[1,1,2,36,32]{3,4,2,0,1:T(8,128)S(1)} collective-permute-done((f32[1,1,2,36,32]{3,4,2,0,1:T(8,128)S(1)}, f32[1,1,2,36,32]{3,4,2,0,1:T(8,128)S(1)}, u32[]{:S(2)}, u32[]{:S(2)}) %collective-permute-start.9) | collective-permute-done | bytes 9248 | tf_op jit(solution)/shard_map/ppermute | solution.py:23
  64.0 3.8 %collective-permute-start.12 = (f32[6,1,2,36,32]{3,4,2,0,1:T(8,128)S(1)}, f32[6,1,2,36,32]{3,4,2,0,1:T(8,128)S(1)}, u32[]{:S(2)}, u32[]{:S(2)}) collective-permute-start(f32[6,1,2,36,32]{3,4,2,0,1:T(8,128)S(1)} %pad_maximum_fusion.6), channel_id=1, source_target_pairs={{2,0},{4,2},{6,4},{0,6},{3,1},{5,3},{7,5},{1,7},{10,8},{12,10},{14... | collective-permute-start | bytes 165896 | tf_op jit(solution)/shard_map/ppermute | solution.py:25
  68.2 3.4 %collective-permute-done.11 = f32[6,1,2,36,32]{3,4,2,0,1:T(8,128)S(1)} collective-permute-done((f32[6,1,2,36,32]{3,4,2,0,1:T(8,128)S(1)}, f32[6,1,2,36,32]{3,4,2,0,1:T(8,128)S(1)}, u32[]{:S(2)}, u32[]{:S(2)}) %collective-permute-start.11) | collective-permute-done | bytes 55328 | tf_op jit(solution)/shard_map/ppermute | solution.py:23
  84.4 1.6 %collective-permute-start.15 = (f32[1,1,2,36,32]{3,4,2,0,1:T(8,128)S(1)}, f32[1,1,2,36,32]{3,4,2,0,1:T(8,128)S(1)}, u32[]{:S(2)}, u32[]{:S(2)}) collective-permute-start(f32[1,1,2,36,32]{3,4,2,0,1:T(8,128)S(1)} %get-tuple-element.51), channel_id=1, source_target_pairs={{0,8},{8,16},{16,24},{24,0},{1,9},{9,17},{17,25},{25,1},{2,10},{10... | collective-permute-start | bytes 27656 | tf_op jit(solution)/shard_map/ppermute | solution.py:23
  86.0 2.0 %collective-permute-done.16 = f32[1,1,2,36,32]{3,4,2,1,0:T(8,128)S(1)} collective-permute-done((f32[1,1,2,36,32]{3,4,2,1,0:T(8,128)S(1)}, f32[1,1,2,36,32]{3,4,2,1,0:T(8,128)S(1)}, u32[]{:S(2)}, u32[]{:S(2)}) %collective-permute-start.16) | collective-permute-done | bytes 9248 | tf_op jit(solution)/shard_map/ppermute | solution.py:25
  90.2 2.9 %collective-permute-start.18 = (f32[6,1,2,36,32]{3,4,2,0,1:T(8,128)S(1)}, f32[6,1,2,36,32]{3,4,2,0,1:T(8,128)S(1)}, u32[]{:S(2)}, u32[]{:S(2)}) collective-permute-start(f32[6,1,2,36,32]{3,4,2,0,1:T(8,128)S(1)} %pad_maximum_fusion.7), channel_id=1, source_target_pairs={{2,0},{4,2},{6,4},{0,6},{3,1},{5,3},{7,5},{1,7},{10,8},{12,10},{14... | collective-permute-start | bytes 165896 | tf_op jit(solution)/shard_map/ppermute | solution.py:25
  93.5 5.4 %collective-permute-done.17 = f32[6,1,2,36,32]{3,4,2,0,1:T(8,128)S(1)} collective-permute-done((f32[6,1,2,36,32]{3,4,2,0,1:T(8,128)S(1)}, f32[6,1,2,36,32]{3,4,2,0,1:T(8,128)S(1)}, u32[]{:S(2)}, u32[]{:S(2)}) %collective-permute-start.17) | collective-permute-done | bytes 55328 | tf_op jit(solution)/shard_map/ppermute | solution.py:23
  115.7 2.3 %collective-permute-done.21 = f32[1,1,2,36,32]{3,4,2,0,1:T(8,128)S(1)} collective-permute-done((f32[1,1,2,36,32]{3,4,2,0,1:T(8,128)S(1)}, f32[1,1,2,36,32]{3,4,2,0,1:T(8,128)S(1)}, u32[]{:S(2)}, u32[]{:S(2)}) %collective-permute-start.21) | collective-permute-done | bytes 9248 | tf_op jit(solution)/shard_map/ppermute | solution.py:23
  118.0 1.7 %collective-permute-start.23 = (f32[6,1,2,36,32]{3,4,2,0,1:T(8,128)S(1)}, f32[6,1,2,36,32]{3,4,2,0,1:T(8,128)S(1)}, u32[]{:S(2)}, u32[]{:S(2)}) collective-permute-start(f32[6,1,2,36,32]{3,4,2,0,1:T(8,128)S(1)} %pad_maximum_fusion.8), channel_id=1, source_target_pairs={{0,2},{2,4},{4,6},{6,0},{1,3},{3,5},{5,7},{7,1},{8,10},{10,12},{12... | collective-permute-start | bytes 165896 | tf_op jit(solution)/shard_map/ppermute | solution.py:23
  119.7 2.2 %collective-permute-start.24 = (f32[6,1,2,36,32]{3,4,2,0,1:T(8,128)S(1)}, f32[6,1,2,36,32]{3,4,2,0,1:T(8,128)S(1)}, u32[]{:S(2)}, u32[]{:S(2)}) collective-permute-start(f32[6,1,2,36,32]{3,4,2,0,1:T(8,128)S(1)} %pad_maximum_fusion.8), channel_id=1, source_target_pairs={{2,0},{4,2},{6,4},{0,6},{3,1},{5,3},{7,5},{1,7},{10,8},{12,10},{14... | collective-permute-start | bytes 165896 | tf_op jit(solution)/shard_map/ppermute | solution.py:25
  122.3 5.3 %collective-permute-done.23 = f32[6,1,2,36,32]{3,4,2,0,1:T(8,128)S(1)} collective-permute-done((f32[6,1,2,36,32]{3,4,2,0,1:T(8,128)S(1)}, f32[6,1,2,36,32]{3,4,2,0,1:T(8,128)S(1)}, u32[]{:S(2)}, u32[]{:S(2)}) %collective-permute-start.23) | collective-permute-done | bytes 55328 | tf_op jit(solution)/shard_map/ppermute | solution.py:23
  127.5 1.6 %collective-permute-done.24 = f32[6,1,2,36,32]{3,4,2,0,1:T(8,128)S(1)} collective-permute-done((f32[6,1,2,36,32]{3,4,2,0,1:T(8,128)S(1)}, f32[6,1,2,36,32]{3,4,2,0,1:T(8,128)S(1)}, u32[]{:S(2)}, u32[]{:S(2)}) %collective-permute-start.24) | collective-permute-done | bytes 55328 | tf_op jit(solution)/shard_map/ppermute | solution.py:25
  (231 shorter events, 69.4 us)
Async XLA Ops:
  3.3 13.4 %collective-permute-start.3 = (f32[1,1,2,4]{3,2,1,0:T(2,128)S(1)}, f32[1,1,2,4]{3,2,1,0:T(2,128)S(1)}, u32[]{:S(2)}, u32[]{:S(2)}) collective-permute-start(f32[1,1,2,4]{3,2,1,0:T(2,128)S(1)} %bitcast.691), channel_id=1, source_target_pairs={{24,0},{0,8},{8,16},{16,24},{25,1},{1,9},{9,17},{17,25},{26,2},{2,... | collective-permute-start | bytes 104 | tf_op jit(solution)/shard_map/ppermute | solution.py:13
  11.7 13.0 %collective-permute-start = (f32[1,1,2,4,3,32]{5,0,4,2,3,1:T(1,128)S(1)}, f32[1,1,2,4,3,32]{5,0,4,2,3,1:T(1,128)S(1)}, u32[]{:S(2)}, u32[]{:S(2)}) collective-permute-start(f32[1,1,2,4,3,32]{5,0,4,2,3,1:T(1,128)S(1)} %copy.129), channel_id=1, source_target_pairs={{24,0},{0,8},{8,16},{16,24},{25,1},{1,9},{9,17},{17,25},{26,2},{2,... | collective-permute-start | bytes 9224 | tf_op jit(solution)/shard_map/ppermute | solution.py:13
  18.0 5.4 %collective-permute-start.4 = (f32[4,1,2,3]{0,2,3,1:T(2,128)S(1)}, f32[4,1,2,3]{0,2,3,1:T(2,128)S(1)}, u32[]{:S(2)}, u32[]{:S(2)}) collective-permute-start(f32[4,1,2,3]{0,2,3,1:T(2,128)S(1)} %bitcast.690), channel_id=1, source_target_pairs={{6,0},{0,2},{2,4},{4,6},{7,1},{1,3},{3,5},{5,7},{14,8},{8,10},{10,... | collective-permute-start | bytes 296 | tf_op jit(solution)/shard_map/ppermute | solution.py:13
  28.2 5.8 %collective-permute-start.1 = (f32[4,1,2,3,3,32]{5,0,4,2,3,1:T(4,128)S(1)}, f32[4,1,2,3,3,32]{5,0,4,2,3,1:T(4,128)S(1)}, u32[]{:S(2)}, u32[]{:S(2)}) collective-permute-start(f32[4,1,2,3,3,32]{5,0,4,2,3,1:T(4,128)S(1)} %bitcast.678), channel_id=1, source_target_pairs={{6,0},{0,2},{2,4},{4,6},{7,1},{1,3},{3,5},{5,7},{14,8},{8,10},{10,... | collective-permute-start | bytes 27656 | tf_op jit(solution)/shard_map/ppermute | solution.py:13
  28.3 9.3 %collective-permute-start.5 = (f32[4,1,1,2]{0,3,2,1:T(2,128)S(1)}, f32[4,1,1,2]{0,3,2,1:T(2,128)S(1)}, u32[]{:S(2)}, u32[]{:S(2)}) collective-permute-start(f32[4,1,1,2]{0,3,2,1:T(2,128)S(1)} %get-tuple-element.59), channel_id=1, source_target_pairs={{1,0},{0,1},{3,2},{2,3},{5,4},{4,5},{7,6},{6,7},{9,8},{8,9},{11,10... | collective-permute-start | bytes 104 | tf_op jit(solution)/shard_map/ppermute | solution.py:13
  44.7 4.0 %collective-permute-start.7 = (f32[4,1,2,3,3,32]{5,0,4,2,3,1:T(4,128)S(1)}, f32[4,1,2,3,3,32]{5,0,4,2,3,1:T(4,128)S(1)}, u32[]{:S(2)}, u32[]{:S(2)}) collective-permute-start(f32[4,1,2,3,3,32]{5,0,4,2,3,1:T(4,128)S(1)} %bitcast.679), channel_id=1, source_target_pairs={{2,0},{4,2},{6,4},{0,6},{3,1},{5,3},{7,5},{1,7},{10,8},{12,10},{14... | collective-permute-start | bytes 27656 | tf_op jit(solution)/shard_map/ppermute | solution.py:13
  50.1 3.7 %collective-permute-start.8 = (f32[1,1,2,4,3,32]{5,0,4,2,3,1:T(1,128)S(1)}, f32[1,1,2,4,3,32]{5,0,4,2,3,1:T(1,128)S(1)}, u32[]{:S(2)}, u32[]{:S(2)}) collective-permute-start(f32[1,1,2,4,3,32]{5,0,4,2,3,1:T(1,128)S(1)} %copy.140), channel_id=1, source_target_pairs={{8,0},{16,8},{24,16},{0,24},{9,1},{17,9},{25,17},{1,25},{10,2},{18... | collective-permute-start | bytes 9224 | tf_op jit(solution)/shard_map/ppermute | solution.py:13
  56.7 4.3 %collective-permute-start.10 = (f32[1,1,2,36,32]{3,4,2,1,0:T(8,128)S(1)}, f32[1,1,2,36,32]{3,4,2,1,0:T(8,128)S(1)}, u32[]{:S(2)}, u32[]{:S(2)}) collective-permute-start(f32[1,1,2,36,32]{3,4,2,1,0:T(8,128)S(1)} %get-tuple-element.54), channel_id=1, source_target_pairs={{8,0},{16,8},{24,16},{0,24},{9,1},{17,9},{25,17},{1,25},{10,2},{18... | collective-permute-start | bytes 27656 | tf_op jit(solution)/shard_map/ppermute | solution.py:25
  59.1 4.8 %collective-permute-start.9 = (f32[1,1,2,36,32]{3,4,2,0,1:T(8,128)S(1)}, f32[1,1,2,36,32]{3,4,2,0,1:T(8,128)S(1)}, u32[]{:S(2)}, u32[]{:S(2)}) collective-permute-start(f32[1,1,2,36,32]{3,4,2,0,1:T(8,128)S(1)} %get-tuple-element.53), channel_id=1, source_target_pairs={{0,8},{8,16},{16,24},{24,0},{1,9},{9,17},{17,25},{25,1},{2,10},{10... | collective-permute-start | bytes 27656 | tf_op jit(solution)/shard_map/ppermute | solution.py:23
  63.9 7.7 %collective-permute-start.11 = (f32[6,1,2,36,32]{3,4,2,0,1:T(8,128)S(1)}, f32[6,1,2,36,32]{3,4,2,0,1:T(8,128)S(1)}, u32[]{:S(2)}, u32[]{:S(2)}) collective-permute-start(f32[6,1,2,36,32]{3,4,2,0,1:T(8,128)S(1)} %pad_maximum_fusion.6), channel_id=1, source_target_pairs={{0,2},{2,4},{4,6},{6,0},{1,3},{3,5},{5,7},{7,1},{8,10},{10,12},{12... | collective-permute-start | bytes 165896 | tf_op jit(solution)/shard_map/ppermute | solution.py:23
  64.0 8.0 %collective-permute-start.12 = (f32[6,1,2,36,32]{3,4,2,0,1:T(8,128)S(1)}, f32[6,1,2,36,32]{3,4,2,0,1:T(8,128)S(1)}, u32[]{:S(2)}, u32[]{:S(2)}) collective-permute-start(f32[6,1,2,36,32]{3,4,2,0,1:T(8,128)S(1)} %pad_maximum_fusion.6), channel_id=1, source_target_pairs={{2,0},{4,2},{6,4},{0,6},{3,1},{5,3},{7,5},{1,7},{10,8},{12,10},{14... | collective-permute-start | bytes 165896 | tf_op jit(solution)/shard_map/ppermute | solution.py:25
  72.1 1.8 %collective-permute-start.13 = (f32[6,3,1,36,32]{3,4,2,0,1:T(8,128)S(1)}, f32[6,3,1,36,32]{3,4,2,0,1:T(8,128)S(1)}, u32[]{:S(2)}, u32[]{:S(2)}) collective-permute-start(f32[6,3,1,36,32]{3,4,2,0,1:T(8,128)S(1)} %get-tuple-element.47), channel_id=1, source_target_pairs={{0,1},{1,0},{2,3},{3,2},{4,5},{5,4},{6,7},{7,6},{8,9},{9,8},{10,11... | collective-permute-start | bytes 248840 | tf_op jit(solution)/shard_map/ppermute | solution.py:23
  72.2 2.0 %collective-permute-start.14 = (f32[6,3,1,36,32]{3,4,2,0,1:T(8,128)S(1)}, f32[6,3,1,36,32]{3,4,2,0,1:T(8,128)S(1)}, u32[]{:S(2)}, u32[]{:S(2)}) collective-permute-start(f32[6,3,1,36,32]{3,4,2,0,1:T(8,128)S(1)} %get-tuple-element.48), channel_id=1, source_target_pairs={{1,0},{0,1},{3,2},{2,3},{5,4},{4,5},{7,6},{6,7},{9,8},{8,9},{11,10... | collective-permute-start | bytes 248840 | tf_op jit(solution)/shard_map/ppermute | solution.py:25
  84.0 4.1 %collective-permute-start.16 = (f32[1,1,2,36,32]{3,4,2,1,0:T(8,128)S(1)}, f32[1,1,2,36,32]{3,4,2,1,0:T(8,128)S(1)}, u32[]{:S(2)}, u32[]{:S(2)}) collective-permute-start(f32[1,1,2,36,32]{3,4,2,1,0:T(8,128)S(1)} %get-tuple-element.52), channel_id=1, source_target_pairs={{8,0},{16,8},{24,16},{0,24},{9,1},{17,9},{25,17},{1,25},{10,2},{18... | collective-permute-start | bytes 27656 | tf_op jit(solution)/shard_map/ppermute | solution.py:25
  84.4 4.8 %collective-permute-start.15 = (f32[1,1,2,36,32]{3,4,2,0,1:T(8,128)S(1)}, f32[1,1,2,36,32]{3,4,2,0,1:T(8,128)S(1)}, u32[]{:S(2)}, u32[]{:S(2)}) collective-permute-start(f32[1,1,2,36,32]{3,4,2,0,1:T(8,128)S(1)} %get-tuple-element.51), channel_id=1, source_target_pairs={{0,8},{8,16},{16,24},{24,0},{1,9},{9,17},{17,25},{25,1},{2,10},{10... | collective-permute-start | bytes 27656 | tf_op jit(solution)/shard_map/ppermute | solution.py:23
  89.3 9.7 %collective-permute-start.17 = (f32[6,1,2,36,32]{3,4,2,0,1:T(8,128)S(1)}, f32[6,1,2,36,32]{3,4,2,0,1:T(8,128)S(1)}, u32[]{:S(2)}, u32[]{:S(2)}) collective-permute-start(f32[6,1,2,36,32]{3,4,2,0,1:T(8,128)S(1)} %pad_maximum_fusion.7), channel_id=1, source_target_pairs={{0,2},{2,4},{4,6},{6,0},{1,3},{3,5},{5,7},{7,1},{8,10},{10,12},{12... | collective-permute-start | bytes 165896 | tf_op jit(solution)/shard_map/ppermute | solution.py:23
  90.2 9.8 %collective-permute-start.18 = (f32[6,1,2,36,32]{3,4,2,0,1:T(8,128)S(1)}, f32[6,1,2,36,32]{3,4,2,0,1:T(8,128)S(1)}, u32[]{:S(2)}, u32[]{:S(2)}) collective-permute-start(f32[6,1,2,36,32]{3,4,2,0,1:T(8,128)S(1)} %pad_maximum_fusion.7), channel_id=1, source_target_pairs={{2,0},{4,2},{6,4},{0,6},{3,1},{5,3},{7,5},{1,7},{10,8},{12,10},{14... | collective-permute-start | bytes 165896 | tf_op jit(solution)/shard_map/ppermute | solution.py:25
  100.2 2.0 %collective-permute-start.20 = (f32[6,3,1,36,32]{3,4,2,0,1:T(8,128)S(1)}, f32[6,3,1,36,32]{3,4,2,0,1:T(8,128)S(1)}, u32[]{:S(2)}, u32[]{:S(2)}) collective-permute-start(f32[6,3,1,36,32]{3,4,2,0,1:T(8,128)S(1)} %get-tuple-element.44), channel_id=1, source_target_pairs={{1,0},{0,1},{3,2},{2,3},{5,4},{4,5},{7,6},{6,7},{9,8},{8,9},{11,10... | collective-permute-start | bytes 248840 | tf_op jit(solution)/shard_map/ppermute | solution.py:25
  111.7 4.0 %collective-permute-start.22 = (f32[1,1,2,36,32]{3,4,2,1,0:T(8,128)S(1)}, f32[1,1,2,36,32]{3,4,2,1,0:T(8,128)S(1)}, u32[]{:S(2)}, u32[]{:S(2)}) collective-permute-start(f32[1,1,2,36,32]{3,4,2,1,0:T(8,128)S(1)} %get-tuple-element.50), channel_id=1, source_target_pairs={{8,0},{16,8},{24,16},{0,24},{9,1},{17,9},{25,17},{1,25},{10,2},{18... | collective-permute-start | bytes 27656 | tf_op jit(solution)/shard_map/ppermute | solution.py:25
  113.2 4.8 %collective-permute-start.21 = (f32[1,1,2,36,32]{3,4,2,0,1:T(8,128)S(1)}, f32[1,1,2,36,32]{3,4,2,0,1:T(8,128)S(1)}, u32[]{:S(2)}, u32[]{:S(2)}) collective-permute-start(f32[1,1,2,36,32]{3,4,2,0,1:T(8,128)S(1)} %get-tuple-element.49), channel_id=1, source_target_pairs={{0,8},{8,16},{16,24},{24,0},{1,9},{9,17},{17,25},{25,1},{2,10},{10... | collective-permute-start | bytes 27656 | tf_op jit(solution)/shard_map/ppermute | solution.py:23
  118.0 9.5 %collective-permute-start.23 = (f32[6,1,2,36,32]{3,4,2,0,1:T(8,128)S(1)}, f32[6,1,2,36,32]{3,4,2,0,1:T(8,128)S(1)}, u32[]{:S(2)}, u32[]{:S(2)}) collective-permute-start(f32[6,1,2,36,32]{3,4,2,0,1:T(8,128)S(1)} %pad_maximum_fusion.8), channel_id=1, source_target_pairs={{0,2},{2,4},{4,6},{6,0},{1,3},{3,5},{5,7},{7,1},{8,10},{10,12},{12... | collective-permute-start | bytes 165896 | tf_op jit(solution)/shard_map/ppermute | solution.py:23
  119.7 9.4 %collective-permute-start.24 = (f32[6,1,2,36,32]{3,4,2,0,1:T(8,128)S(1)}, f32[6,1,2,36,32]{3,4,2,0,1:T(8,128)S(1)}, u32[]{:S(2)}, u32[]{:S(2)}) collective-permute-start(f32[6,1,2,36,32]{3,4,2,0,1:T(8,128)S(1)} %pad_maximum_fusion.8), channel_id=1, source_target_pairs={{2,0},{4,2},{6,4},{0,6},{3,1},{5,3},{7,5},{1,7},{10,8},{12,10},{14... | collective-permute-start | bytes 165896 | tf_op jit(solution)/shard_map/ppermute | solution.py:25
  129.3 1.7 %collective-permute-start.25 = (f32[6,3,1,36,32]{3,4,2,0,1:T(8,128)S(1)}, f32[6,3,1,36,32]{3,4,2,0,1:T(8,128)S(1)}, u32[]{:S(2)}, u32[]{:S(2)}) collective-permute-start(f32[6,3,1,36,32]{3,4,2,0,1:T(8,128)S(1)} %get-tuple-element.39), channel_id=1, source_target_pairs={{0,1},{1,0},{2,3},{3,2},{4,5},{5,4},{6,7},{7,6},{8,9},{9,8},{10,11... | collective-permute-start | bytes 248840 | tf_op jit(solution)/shard_map/ppermute | solution.py:23
  129.3 2.0 %collective-permute-start.26 = (f32[6,3,1,36,32]{3,4,2,0,1:T(8,128)S(1)}, f32[6,3,1,36,32]{3,4,2,0,1:T(8,128)S(1)}, u32[]{:S(2)}, u32[]{:S(2)}) collective-permute-start(f32[6,3,1,36,32]{3,4,2,0,1:T(8,128)S(1)} %get-tuple-element.40), channel_id=1, source_target_pairs={{1,0},{0,1},{3,2},{2,3},{5,4},{4,5},{7,6},{6,7},{9,8},{8,9},{11,10... | collective-permute-start | bytes 248840 | tf_op jit(solution)/shard_map/ppermute | solution.py:25
  (24 other events, 189.9 us)
where the time goes:
time: 142 us
  waiting for transfers between devices  45.3 us (32%)
  matrix products  36 us (25%)
  starting transfers between devices  28.1 us (20%)
  local copies, waits for them, and re-layouts  18.7 us (13%)
  other arithmetic  11.5 us (8%)
  between operations  2.03 us (1%)
    dot_general x81, matrix products, apply_matrix(): jnp.einsum('xyzij,xyzjr->xyzir', coarse_matrix[:, :, :, offset], piece, p...  30.6 us
    ppermute x9, waiting for transfers between devices, with_halo(): lax.ppermute(tail, axis, [(i, (i + 1) % count) for i in range(count)])  20.4 us
    ppermute x9, waiting for transfers between devices, passed_along(): return lax.ppermute(block, axis, route)  17.2 us
    ppermute x9, starting transfers between devices, with_halo(): lax.ppermute(head, axis, [((i + 1) % count, i) for i in range(count)])  14.7 us
    ppermute x9, starting transfers between devices, passed_along(): return lax.ppermute(block, axis, route)  8.07 us
    ppermute x9, waiting for transfers between devices, with_halo(): lax.ppermute(head, axis, [((i + 1) % count, i) for i in range(count)])  7.64 us
    ppermute x9, starting transfers between devices, with_halo(): lax.ppermute(tail, axis, [(i, (i + 1) % count) for i in range(count)])  5.31 us
    slice x2, local copies, waits for them, and re-layouts, apply_matrix(): coarse_matrix[:, :, :, offset]  4.62 us
  transfers between devices with their start and end apart: 27, of which 21 were waited for; matrix products, arithmetic and copies ran while one was open for 16% of the time, Pallas kernels for 0%

commit v1 on v0

v1 whole, which is shorter than its diff:
```python
import functools
import itertools

import jax
import jax.numpy as jnp
import ml_dtypes
import numpy as np
from jax import lax
from jax.experimental import pallas as pl
from jax.experimental.pallas import tpu as pltpu
from jax.sharding import PartitionSpec as P

SWEEPS = 4
MESH = pl.DeviceIdType.MESH
F32 = jnp.float32
BF16 = jnp.bfloat16
OFFSETS = [
    (0, 0, 0), (0, 0, 1), (0, 1, 0), (0, 1, 1),
    (0, 0, 0), (0, 0, 1), (1, 0, 0), (1, 0, 1),
    (0, 0, 0), (0, 1, 0), (1, 0, 0), (1, 1, 0),
]
STEPS = [(0, 0)] + [s for s in itertools.product((-1, 0, 1), (-1, 0, 1)) if s != (0, 0)]
SLOT = {s: i for i, s in enumerate(STEPS)}
HALF = 48


def site_row(edge, comp):
    oy = OFFSETS[edge][1]
    if edge < 4:
        return 3 * oy + comp
    if edge < 8:
        return (6, 7, 14)[comp]
    return 8 + 3 * oy + comp


def tables():
    place = np.zeros((36, 64), np.float32)
    spread = np.zeros((64, 12), np.float32)
    chunk = np.full((64, 128), -1, np.int32)
    fold = np.zeros((3, 108, 256), np.float32)
    order = np.zeros((HALF, 36), np.float32)
    rest = 16
    for edge in range(12):
        ox, oy, oz = OFFSETS[edge]
        for comp in range(3):
            row = 3 * edge + comp
            site = site_row(edge, comp)
            wide = 16 * (2 * ox + oz) + site
            place[row, wide] = 1
            spread[wide, edge] = 1
            chunk[wide] = row - np.arange(128) // 32
            for dx in range(3):
                for dz in range(3):
                    fold[dx, 36 * dz + row, 64 * (dx + ox) + 16 * (dz + oz) + site] = 1
            if ox == 0 and oz == 0:
                order[site, row] = 1
            else:
                order[rest, row] = 1
                rest += 1
    kind = ml_dtypes.bfloat16
    return (place.astype(kind), spread.astype(kind), chunk, fold.astype(kind),
            order.astype(kind), np.ascontiguousarray(order.T).astype(kind))


def split(value):
    high = value.astype(BF16)
    return high, (value - high.astype(F32)).astype(BF16)


def dot(a, b):
    return jnp.dot(a, b, preferred_element_type=F32)


def kernel(sizes, disp_hbm, weight_ref, matrix_hbm, inverse_ref, place_ref, spread_ref, chunk_ref,
           fold_ref, order_ref, back_ref, average_ref, result_ref,
           disp, matrix, operator, main, rim, zsend, zgot, sites, below, above, rows, wide,
           load_sem, send_sem, got_sem):
    nx, nz = 4, 2
    gx, gy, gz = (lax.axis_index(a) for a in ("gx", "gy", "gz"))
    cx, cy, cz = sizes

    def at(dx, dy, dz):
        return (lax.rem(gx + dx + cx, cx), lax.rem(gy + dy + cy, cy), lax.rem(gz + dz + cz, cz))

    load_disp = pltpu.make_async_copy(disp_hbm, disp, load_sem.at[0])
    load_matrix = pltpu.make_async_copy(matrix_hbm, matrix, load_sem.at[1])
    load_disp.start()
    load_matrix.start()
    barrier = pltpu.get_barrier_semaphore()
    for dx, dy in STEPS[1:]:
        pl.semaphore_signal(barrier, inc=1, device_id=at(dx, dy, 0), device_id_type=MESH)
    for dz in (-1, 1):
        pl.semaphore_signal(barrier, inc=1, device_id=at(0, 0, dz), device_id_type=MESH)

    lane = lax.broadcasted_iota(jnp.int32, (16, 128), 1)
    row = lax.broadcasted_iota(jnp.int32, (16, 128), 0)
    part = lane // 32
    ones = jnp.ones((128, 128), BF16)
    zero = jnp.zeros((16, 128), F32)

    load_disp.wait()
    number = {}
    mass = {}
    for cell in range(nx * nz):
        weight = dot(spread_ref[...], weight_ref[cell]).astype(BF16)
        full = lax.dot_general(weight, disp[cell], (((1,), (1,)), ((), ())),
                               preferred_element_type=F32)
        total = jnp.zeros((64, 128), F32)
        for t in range(9):
            total = total + jnp.where(chunk_ref[...] == 4 * t, full[:, 128 * t:128 * t + 128], 0.0)
        total = total + pltpu.roll(total, 64, 1)
        total = total + pltpu.roll(total, 32, 1)
        number[cell] = total
        mass[cell] = dot(weight, ones)
    for zs in range(nz + 1):
        body = zero
        edge = zero
        for oz in range(2):
            z = zs - oz
            if not 0 <= z < nz:
                continue
            for x in range(nx):
                for ox in range(2):
                    b = 16 * (2 * ox + oz)
                    value = number[x * nz + z][b:b + 16]
                    if x + ox < nx:
                        body = body + jnp.where(part == x + ox, value, 0.0)
                    else:
                        edge = edge + jnp.where(part == 0, value, 0.0)
                    heavy = mass[x * nz + z][b:b + 16]
                    edge = edge + jnp.where(lane // 8 == 4 + x + ox, heavy, 0.0)
        main[1, zs] = body
        rim[0, zs] = edge + jnp.where(part == 3, pltpu.roll(body, 96, 1), 0.0)

    pl.semaphore_wait(barrier, 10)
    copies = []
    for i, (dx, dy) in enumerate(STEPS):
        if i == 0:
            continue
        slot = SLOT[(-dx, -dy)]
        copies.append(pltpu.make_async_remote_copy(
            rim.at[0], rim.at[slot], send_sem.at[0, i], got_sem.at[0, slot],
            device_id=at(dx, dy, 0), device_id_type=MESH))
        if dx == 0:
            copies.append(pltpu.make_async_remote_copy(
                main.at[1], main.at[1 - dy], send_sem.at[0, 11 + (dy + 1) // 2],
                got_sem.at[0, 11 + (1 - dy) // 2],
                device_id=at(dx, dy, 0), device_id_type=MESH))
    for copy in copies:
        copy.start()

    load_matrix.wait()

    def prepare(cell, carry):
        base_high, base_low = split(inverse_ref[cell])
        base_high = dot(order_ref[...], base_high).astype(BF16)
        base_low = dot(order_ref[...], base_low).astype(BF16)
        for dy in range(3):
            sum_high = jnp.zeros((36, 256), F32)
            sum_low = jnp.zeros((36, 256), F32)
            for dx in range(3):
                first = 27 * cell + 9 * dx + 3 * dy
                joined = jnp.concatenate([matrix[first + k] for k in range(3)], axis=1)
                high, low = split(joined)
                sum_high = sum_high + dot(high, fold_ref[dx])
                sum_low = sum_low + dot(low, fold_ref[dx])
            sum_high = sum_high.astype(BF16)
            sum_low = sum_low.astype(BF16)
            scaled = dot(base_high, sum_high) + dot(base_low, sum_high) + dot(base_high, sum_low)
            high, low = split(scaled)
            operator[cell, dy, :HALF] = high
            operator[cell, dy, HALF:] = low
        return carry

    lax.fori_loop(0, nx * nz, prepare, 0)

    for copy in copies:
        copy.wait()

    lower = (row % 8) < 3
    upper = ((row % 8) >= 3) & ((row % 8) < 6)
    for zs in range(nz + 1):
        sums = {}
        for dy in (-1, 0, 1):
            before = rim[SLOT[(-1, dy)], zs]
            after = pltpu.roll(rim[SLOT[(1, dy)], zs], 32, 1)
            body = main[1 + dy, zs] + jnp.where(part == 0, before, 0.0)
            edge = (rim[SLOT[(0, dy)], zs]
                    + jnp.where(lane // 8 == 4, pltpu.roll(before, 96, 1), 0.0)
                    + jnp.where((part == 0) | (lane // 8 == 8), after, 0.0))
            sums[dy] = (body, edge)
        for k in range(2):
            zsend[zs, k] = (sums[0][k]
                            + jnp.where(lower, pltpu.roll(sums[-1][k], 13, 0), 0.0)
                            + jnp.where(upper, pltpu.roll(sums[1][k], 3, 0), 0.0))
    copies = [
        pltpu.make_async_remote_copy(zsend.at[nz], zgot.at[0], send_sem.at[0, 9], got_sem.at[0, 9],
                                     device_id=at(0, 0, 1), device_id_type=MESH),
        pltpu.make_async_remote_copy(zsend.at[0], zgot.at[1], send_sem.at[0, 10], got_sem.at[0, 10],
                                     device_id=at(0, 0, -1), device_id_type=MESH),
    ]
    for copy in copies:
        copy.start()
    for copy in copies:
        copy.wait()
    inner = []
    outer = []
    for zs in range(nz + 1):
        body = zsend[zs, 0]
        edge = zsend[zs, 1]
        if zs == 0:
            body, edge = body + zgot[0, 0], edge + zgot[0, 1]
        if zs == nz:
            body, edge = body + zgot[1, 0], edge + zgot[1, 1]
        heavy = zero
        for x in range(nx):
            heavy = jnp.where(part == x, edge[:, 32 + 8 * x:33 + 8 * x], heavy)
        last = jnp.broadcast_to(edge[:, 64:65], (16, 128))
        inner.append(body / jnp.where(heavy == 0.0, 1.0, heavy))
        edge = edge / jnp.where(last == 0.0, 1.0, last)
        outer.append(jnp.where(part == 3, pltpu.roll(edge, 96, 1), pltpu.roll(inner[-1], 96, 1)))

    def joined_split(value):
        high, low = split(value)
        return jnp.concatenate([high, low], axis=1)

    def store(ref, z, value):
        for x in range(nx):
            ref[x * nz + z] = value[:, 32 * x:32 * x + 32]

    wide_part = lax.broadcasted_iota(jnp.int32, (HALF, 128), 1) // 32
    start = []
    current = []
    for z in range(nz):
        wide[...] = jnp.concatenate([inner[z], inner[z + 1], outer[z], outer[z + 1]], axis=0)
        pair = joined_split(wide[...])
        cells = dot(place_ref[...], pair)
        cells = cells[:, :128] + cells[:, 128:]
        store(average_ref, z, cells)
        pair = joined_split(cells)
        value = jnp.zeros((HALF, 128), F32)
        for x in range(nx):
            base_high, base_low = split(inverse_ref[x * nz + z])
            base_high = dot(order_ref[...], base_high).astype(BF16)
            base_low = dot(order_ref[...], base_low).astype(BF16)
            whole = dot(base_high, pair)
            whole = whole[:, :128] + whole[:, 128:] + dot(base_low, pair[:, :128])
            value = jnp.where(wide_part == x, whole, value)
        start.append(value)
        current.append(value)

    for sweep in range(SWEEPS - 1):
        r = sweep + 1
        for z in range(nz):
            sites[sweep, 0, z] = current[z][:16]
        copies = []
        for i, (dx, dy) in enumerate(STEPS):
            if i == 0:
                continue
            slot = SLOT[(-dx, -dy)]
            copies.append(pltpu.make_async_remote_copy(
                sites.at[sweep, 0], sites.at[sweep, slot], send_sem.at[r, i], got_sem.at[r, slot],
                device_id=at(dx, dy, 0), device_id_type=MESH))
        for copy in copies:
            copy.start()
        for copy in copies:
            copy.wait()
        copies = [
            pltpu.make_async_remote_copy(
                sites.at[sweep, :, nz - 1], below.at[sweep], send_sem.at[r, 9], got_sem.at[r, 9],
                device_id=at(0, 0, 1), device_id_type=MESH),
            pltpu.make_async_remote_copy(
                sites.at[sweep], above.at[sweep], send_sem.at[r, 10], got_sem.at[r, 10],
                device_id=at(0, 0, -1), device_id_type=MESH),
        ]
        for copy in copies:
            copy.start()

        def gather(zs, load, sweep=sweep):
            for dy in (-1, 0, 1):
                own, before, after = (load(SLOT[(s, dy)]) for s in (0, -1, 1))
                shifted = [
                    jnp.where(part == 0, pltpu.roll(before, 32, 1), pltpu.roll(own, 32, 1)),
                    own,
                    jnp.where(part == 3, pltpu.roll(after, 96, 1), pltpu.roll(own, 96, 1)),
                    jnp.where(part >= 2, pltpu.roll(after, 64, 1), pltpu.roll(own, 64, 1)),
                ]
                for s in range(4):
                    high, low = split(shifted[s])
                    rows[dy + 1, s, zs, :, :128] = high
                    rows[dy + 1, s, zs, :, 128:] = low

        for z in range(nz):
            gather(1 + z, lambda slot, z=z: sites[sweep, slot, z])
        for copy in copies:
            copy.wait()
        gather(0, lambda slot: below[sweep, slot])
        for z in range(2):
            gather(3 + z, lambda slot, z=z: above[sweep, slot, z])
        for z in range(nz):
            product = [jnp.zeros((2 * HALF, 256), F32) for _ in range(nx)]
            for dy in range(3):
                right = rows[dy, :, z:z + 4].reshape(256, 256)
                left = jnp.concatenate([operator[x * nz + z, dy] for x in range(nx)], axis=0)
                whole = dot(left, right)
                for x in range(nx):
                    product[x] = product[x] + whole[2 * HALF * x:2 * HALF * (x + 1)]
            value = jnp.zeros((HALF, 128), F32)
            for x in range(nx):
                whole = product[x][:HALF, :128] + product[x][:HALF, 128:] + product[x][HALF:, :128]
                value = jnp.where(wide_part == x, whole, value)
            current[z] = start[z] + (current[z] - value)

    for z in range(nz):
        cells = dot(back_ref[...], joined_split(current[z]))
        store(result_ref, z, cells[:, :128] + cells[:, 128:])


def body(sizes, displacement, dof_weight, coarse_matrix, block_inverse):
    shape = displacement.shape
    cells = shape[0] * shape[1] * shape[2]
    edges = shape[3]
    rhs, dofs = shape[5], shape[6]
    coarse = block_inverse.shape[-1]
    consts = [jnp.asarray(t) for t in tables()]
    vmem = pl.BlockSpec(memory_space=pltpu.VMEM)
    hbm = pl.BlockSpec(memory_space=pl.ANY)
    average, result = pl.pallas_call(
        functools.partial(kernel, sizes),
        out_shape=[jax.ShapeDtypeStruct((cells, coarse, rhs), F32)] * 2,
        in_specs=[hbm, vmem, hbm] + [vmem] * 7,
        out_specs=[vmem, vmem],
        scratch_shapes=[
            pltpu.VMEM((cells, 3 * edges * rhs, dofs), BF16),
            pltpu.VMEM((27 * cells, coarse, coarse), F32),
            pltpu.VMEM((cells, 3, 2 * HALF, 256), BF16),
            pltpu.VMEM((3, 3, 16, 128), F32),
            pltpu.VMEM((9, 3, 16, 128), F32),
            pltpu.VMEM((3, 2, 16, 128), F32),
            pltpu.VMEM((2, 2, 16, 128), F32),
            pltpu.VMEM((SWEEPS - 1, 9, 2, 16, 128), F32),
            pltpu.VMEM((SWEEPS - 1, 9, 16, 128), F32),
            pltpu.VMEM((SWEEPS - 1, 9, 2, 16, 128), F32),
            pltpu.VMEM((3, 4, 5, 16, 256), BF16),
            pltpu.VMEM((64, 128), F32),
            pltpu.SemaphoreType.DMA((2,)),
            pltpu.SemaphoreType.DMA((SWEEPS, 13)),
            pltpu.SemaphoreType.DMA((SWEEPS, 13)),
        ],
        compiler_params=pltpu.CompilerParams(
            collective_id=0, has_side_effects=True, vmem_limit_bytes=40 * 1024 * 1024
        ),
    )(
        displacement.reshape(cells, 3 * edges * rhs, dofs),
        dof_weight.reshape(cells, edges, dofs),
        coarse_matrix.reshape(27 * cells, coarse, coarse),
        block_inverse.reshape(cells, coarse, coarse),
        *consts,
    )
    return (
        average.reshape(shape[:3] + (edges, 3, rhs)),
        result.reshape(shape[:3] + (coarse, rhs)),
    )


def solution(mesh):
    placed = (
        P("gx", "gy", "gz", None, None, None, None),
        P("gx", "gy", "gz", None, None),
        P("gx", "gy", "gz", None, None, None),
        P("gx", "gy", "gz", None, None),
    )
    sizes = tuple(mesh.shape[a] for a in ("gx", "gy", "gz"))
    return jax.shard_map(
        functools.partial(body, sizes),
        mesh=mesh,
        in_specs=placed,
        out_specs=(P("gx", "gy", "gz", None, None, None), P("gx", "gy", "gz", None, None)),
        check_vma=False,
    )
```

time: 142 us -> 47.5 us (0.33)
  waiting for transfers between devices: 45.3 us -> 0 us
  Pallas kernels: 0 us -> 40.5 us
  matrix products: 36 us -> 0 us
  starting transfers between devices: 28.1 us -> 0 us
  local copies, waits for them, and re-layouts: 18.7 us -> 6.01 us
  other arithmetic: 11.5 us -> 0 us
    ppermute x27 -> x0, waiting for transfers between devices: 45.3 us -> none  [the longest x9 20.4 us: with_halo(): lax.ppermute(tail, axis, [(i, (i + 1) % count) for i in range(count)])]
    pallas_call x0 -> x1, Pallas kernels: none -> 40.5 us  [body(): pl.pallas_call(functools.partial(kernel, sizes), out_shape=[jax.ShapeDtyp...]
    dot_general x86 -> x0, matrix products: 36 us -> none  [the longest x81 30.6 us: apply_matrix(): jnp.einsum('xyzij,xyzjr->xyzir', coarse_matrix[:, :, :, offset], piece, p...]
    ppermute x27 -> x0, starting transfers between devices: 28.1 us -> none  [the longest x9 14.7 us: with_halo(): lax.ppermute(head, axis, [((i + 1) % count, i) for i in range(count)])]
    gather x10 -> x0, local copies, waits for them, and re-layouts: 7.91 us -> none  [the longest x3 4.46 us: body(): moving_numer = numers[:, :, :, sources]]
    scatter-add x6 -> x0, other arithmetic: 7.75 us -> none  [the longest x1 2 us: body(): numers.at[:, :, :, targets].add(from_below(moving_numer, got_numer, 0))]
    slice x22 -> x0, local copies, waits for them, and re-layouts: 5.14 us -> none  [the longest x2 4.62 us: apply_matrix(): coarse_matrix[:, :, :, offset]]
    unnamed x43 -> x19, local copies, waits for them, and re-layouts: 0.85 us -> 5.98 us
  transfers between devices with their start and end apart: 27 -> 0, of which waited for: 21 -> 0; matrix products, arithmetic and copies ran while one was open for 16% -> 0% of each run, Pallas kernels for 0% -> 0%
where the time goes in v1:
time: 47.5 us; the launch traced here: 47.3 us
  Pallas kernels  40.5 us (85%)
  local copies, waits for them, and re-layouts  6.01 us (13%)
  between operations  0.73 us (2%)
    pallas_call x1, Pallas kernels, body(): pl.pallas_call(functools.partial(kernel, sizes), out_shape=[jax.ShapeDtyp...  40.5 us
    unnamed x19, local copies, waits for them, and re-layouts  5.98 us

profile of v1, /device:TPU:0, one launch (start us, length us, event | category | flops | bytes accessed | tf_op | source)
XLA Modules:
  0.0 47.3 jit_solution(10730869602951492251)
XLA Ops:
  0.6 0.7 %copy.17 = bf16[4,1,2,12,128]{4,3,2,0,1:T(8,128)(2,1)S(1)} copy(bf16[4,1,2,12,128]{4,2,3,1,0:T(2,128)(2,1)} %param.11) | data formatting | bytes 49152 | tf_op args[1]
  1.4 0.9 %copy.19 = f32[4,1,2,36,36]{4,3,2,0,1:T(8,128)S(1)} copy(f32[4,1,2,36,36]{4,2,3,1,0:T(2,128)} %param.13) | data formatting | bytes 82944 | tf_op args[3]
  2.3 0.0 copy-start
  2.3 0.0 copy-start.1
  2.3 0.0 copy-start.2
  2.3 0.0 copy-start.3
  2.4 0.0 copy-start.4
  2.4 0.0 copy-start.5
  2.4 0.0 copy-start.6
  2.4 2.6 %copy.18 = f32[4,1,2,27,36,36]{5,4,3,2,0,1:T(8,128)S(1)} copy(f32[4,1,2,27,36,36]{5,2,4,3,1,0:T(2,128)} %param.12) | data formatting | bytes 2239488 | tf_op args[2]
  5.0 0.2 copy-done
  5.2 0.0 copy-done.1
  5.2 0.0 copy-done.2
  5.2 0.0 copy-done.3
  5.2 0.0 copy-done.4
  5.2 0.0 copy-done.5
  5.2 0.0 copy-done.6
  5.2 40.5 %shard_map.113 = (f32[8,36,32]{2,1,0:T(8,128)S(1)}, f32[8,36,32]{2,1,0:T(8,128)S(1)}) custom-call(bf16[8,1152,128]{2,1,0:T(8,128)(2,1)S(1)} %bitcast.7, bf16[8,12,128]{2,1,0:T(8,128)(2,1)S(1)} %bitcast.10, f32[216,36,36]{2,1,0:T(8,128)S(1)} %bitcast.6, f32[8,36,36]{2,1,0:T(8,128)S(1)} %bitcast.8, bf16[36,64]{1,0:T(8,128)(2,1)S(1)} %copy-done.6, ...), custom_call_target="tpu_custom_call" | custom-call | tf_op jit(solution)/shard_map/pallas_call | solution.py:328
  45.8 0.7 %copy.21 = f32[4,1,2,12,3,32]{5,2,4,3,1,0:T(2,128)} copy(f32[4,1,2,12,3,32]{5,2,0,4,3,1:T(2,128)S(1)} %bitcast.11) | data formatting | bytes 73728
  46.5 0.8 %copy.22 = f32[4,1,2,36,32]{3,4,2,1,0:T(8,128)} copy(f32[4,1,2,36,32]{4,3,2,0,1:T(8,128)S(1)} %bitcast.9) | data formatting | bytes 73728
  (1 shorter events, 0.0 us)
Async XLA Ops:
  2.3 2.9 %copy-start = (bf16[4,1,2,12,3,32,128]{6,5,4,3,2,1,0:T(8,128)(2,1)S(1)}, bf16[4,1,2,12,3,32,128]{6,5,4,3,2,1,0:T(8,128)(2,1)}, u32[]{:S(2)}) copy-start(bf16[4,1,2,12,3,32,128]{6,5,4,3,2,1,0:T(8,128)(2,1)} %param.10) | copy-start | bytes 7077892
  2.3 2.9 %copy-start.1 = (bf16[3,108,256]{2,1,0:T(8,128)(2,1)S(1)}, bf16[3,108,256]{2,1,0:T(8,128)(2,1)}, u32[]{:S(2)}) copy-start(bf16[3,108,256]{2,1,0:T(8,128)(2,1)} %constant.15.clone.fold_ref) | copy-start | bytes 497668
  2.3 2.8 %copy-start.2 = (s32[64,128]{1,0:T(8,128)S(1)}, s32[64,128]{1,0:T(8,128)}, u32[]{:S(2)}) copy-start(s32[64,128]{1,0:T(8,128)} %constant.14.clone.chunk_ref) | copy-start | bytes 98308
  2.3 2.8 %copy-start.3 = (bf16[64,12]{1,0:T(8,128)(2,1)S(1)}, bf16[64,12]{1,0:T(8,128)(2,1)}, u32[]{:S(2)}) copy-start(bf16[64,12]{1,0:T(8,128)(2,1)} %constant.13.clone.spread_ref) | copy-start | bytes 4612
  2.4 2.8 %copy-start.4 = (bf16[48,36]{1,0:T(8,128)(2,1)S(1)}, bf16[48,36]{1,0:T(8,128)(2,1)}, u32[]{:S(2)}) copy-start(bf16[48,36]{1,0:T(8,128)(2,1)} %constant.16.clone.order_ref) | copy-start | bytes 10372
  2.4 2.8 %copy-start.5 = (bf16[36,48]{1,0:T(8,128)(2,1)S(1)}, bf16[36,48]{1,0:T(8,128)(2,1)}, u32[]{:S(2)}) copy-start(bf16[36,48]{1,0:T(8,128)(2,1)} %constant.17.clone.back_ref) | copy-start | bytes 10372
  2.4 2.8 %copy-start.6 = (bf16[36,64]{1,0:T(8,128)(2,1)S(1)}, bf16[36,64]{1,0:T(8,128)(2,1)}, u32[]{:S(2)}) copy-start(bf16[36,64]{1,0:T(8,128)(2,1)} %constant.12.clone.place_ref) | copy-start | bytes 13828

commit v2 on v1

--- a/solution.py
+++ b/solution.py
@@ -22,6 +22,7 @@
 STEPS = [(0, 0)] + [s for s in itertools.product((-1, 0, 1), (-1, 0, 1)) if s != (0, 0)]
 SLOT = {s: i for i, s in enumerate(STEPS)}
 HALF = 48
+PAIR = 80
 
 
 def site_row(edge, comp):
@@ -33,12 +34,13 @@
     return 8 + 3 * oy + comp
 
 
-def tables():
-    place = np.zeros((36, 64), np.float32)
-    spread = np.zeros((64, 12), np.float32)
+def tables(nz):
+    place = np.zeros((36 * nz, 64 * nz), np.float32)
+    spread = np.zeros((nz, 64, 12 * nz), np.float32)
     chunk = np.full((64, 128), -1, np.int32)
     fold = np.zeros((3, 108, 256), np.float32)
     order = np.zeros((HALF, 36), np.float32)
+    widen = np.zeros((2, nz, 36, 3 * PAIR), np.float32)
     rest = 16
     for edge in range(12):
         ox, oy, oz = OFFSETS[edge]
@@ -46,9 +48,13 @@
             row = 3 * edge + comp
             site = site_row(edge, comp)
             wide = 16 * (2 * ox + oz) + site
-            place[row, wide] = 1
-            spread[wide, edge] = 1
             chunk[wide] = row - np.arange(128) // 32
+            for z in range(nz):
+                place[nz * row + z, 64 * z + wide] = 1
+                spread[z, wide, nz * edge + z] = 1
+                widen[0, z, row, nz * row + z] = 1
+                widen[1, z, row, PAIR + nz * row + z] = 1
+                widen[0, z, row, 2 * PAIR + nz * row + z] = 1
             for dx in range(3):
                 for dz in range(3):
                     fold[dx, 36 * dz + row, 64 * (dx + ox) + 16 * (dz + oz) + site] = 1
@@ -59,7 +65,7 @@
                 rest += 1
     kind = ml_dtypes.bfloat16
     return (place.astype(kind), spread.astype(kind), chunk, fold.astype(kind),
-            order.astype(kind), np.ascontiguousarray(order.T).astype(kind))
+            order.astype(kind), widen.astype(kind))
 
 
 def split(value):
@@ -72,9 +78,9 @@
 
 
 def kernel(sizes, disp_hbm, weight_ref, matrix_hbm, inverse_ref, place_ref, spread_ref, chunk_ref,
-           fold_ref, order_ref, back_ref, average_ref, result_ref,
-           disp, matrix, operator, main, rim, zsend, zgot, sites, below, above, rows, wide,
-           load_sem, send_sem, got_sem):
+           fold_ref, order_ref, widen_ref, average_ref, result_ref,
+           disp, matrix, operator, main, rim, zsend, zgot, sites, below, above, rows, wide, base, cells_ref,
+           load_sem, send_sem, got_sem, pass_sem, passed_sem):
     nx, nz = 4, 2
     gx, gy, gz = (lax.axis_index(a) for a in ("gx", "gy", "gz"))
     cx, cy, cz = sizes
@@ -102,7 +108,7 @@
     number = {}
     mass = {}
     for cell in range(nx * nz):
-        weight = dot(spread_ref[...], weight_ref[cell]).astype(BF16)
+        weight = dot(spread_ref[cell % nz], weight_ref[cell // nz]).astype(BF16)
         full = lax.dot_general(weight, disp[cell], (((1,), (1,)), ((), ())),
                                preferred_element_type=F32)
         total = jnp.zeros((64, 128), F32)
@@ -151,28 +157,33 @@
 
     load_matrix.wait()
 
-    def prepare(cell, carry):
-        base_high, base_low = split(inverse_ref[cell])
-        base_high = dot(order_ref[...], base_high).astype(BF16)
-        base_low = dot(order_ref[...], base_low).astype(BF16)
+    def prepare(x, carry):
+        wide_base = []
+        for z in range(nz):
+            high, low = split(inverse_ref[x, pl.ds(z, 36, stride=nz), :])
+            high = dot(order_ref[...], high).astype(BF16)
+            low = dot(order_ref[...], low).astype(BF16)
+            base[z, x, :HALF] = high
+            base[z, x, HALF:] = low
+            wide_base.append(dot(high, widen_ref[0, z]) + dot(low, widen_ref[1, z]))
+        wide_base = jnp.concatenate(wide_base, axis=0).astype(BF16)
         for dy in range(3):
-            sum_high = jnp.zeros((36, 256), F32)
-            sum_low = jnp.zeros((36, 256), F32)
+            total = jnp.zeros((2 * PAIR, 256), F32)
             for dx in range(3):
-                first = 27 * cell + 9 * dx + 3 * dy
+                first = 27 * x + 9 * dx + 3 * dy
                 joined = jnp.concatenate([matrix[first + k] for k in range(3)], axis=1)
-                high, low = split(joined)
-                sum_high = sum_high + dot(high, fold_ref[dx])
-                sum_low = sum_low + dot(low, fold_ref[dx])
-            sum_high = sum_high.astype(BF16)
-            sum_low = sum_low.astype(BF16)
-            scaled = dot(base_high, sum_high) + dot(base_low, sum_high) + dot(base_high, sum_low)
-            high, low = split(scaled)
-            operator[cell, dy, :HALF] = high
-            operator[cell, dy, HALF:] = low
+                joined = jnp.concatenate([joined, jnp.zeros((PAIR - 36 * nz, 108), F32)], axis=0)
+                total = total + dot(jnp.concatenate(split(joined), axis=0), fold_ref[dx])
+            total = total.astype(BF16)
+            total = jnp.concatenate([total[:PAIR], total[:PAIR], total[PAIR:]], axis=0)
+            scaled = dot(wide_base, total)
+            for z in range(nz):
+                high, low = split(scaled[HALF * z:HALF * (z + 1)])
+                operator[z, dy, x, :HALF] = high
+                operator[z, dy, x, HALF:] = low
         return carry
 
-    lax.fori_loop(0, nx * nz, prepare, 0)
+    lax.fori_loop(0, nx, prepare, 0)
 
     for copy in copies:
         copy.wait()
@@ -224,28 +235,25 @@
         high, low = split(value)
         return jnp.concatenate([high, low], axis=1)
 
-    def store(ref, z, value):
-        for x in range(nx):
-            ref[x * nz + z] = value[:, 32 * x:32 * x + 32]
-
     wide_part = lax.broadcasted_iota(jnp.int32, (HALF, 128), 1) // 32
     start = []
     current = []
     for z in range(nz):
-        wide[...] = jnp.concatenate([inner[z], inner[z + 1], outer[z], outer[z + 1]], axis=0)
-        pair = joined_split(wide[...])
-        cells = dot(place_ref[...], pair)
-        cells = cells[:, :128] + cells[:, 128:]
-        store(average_ref, z, cells)
-        pair = joined_split(cells)
+        wide[z] = jnp.concatenate([inner[z], inner[z + 1], outer[z], outer[z + 1]], axis=0)
+    pair = joined_split(wide[...].reshape(64 * nz, 128))
+    cells = dot(place_ref[...], pair)
+    cells = cells[:, :128] + cells[:, 128:]
+    for x in range(nx):
+        average_ref[x] = cells[:, 32 * x:32 * x + 32]
+    cells_ref[...] = cells
+    for z in range(nz):
+        right = joined_split(cells_ref[pl.ds(z, 36, stride=nz), :])
+        whole = dot(base[z].reshape(2 * HALF * nx, 36), right)
         value = jnp.zeros((HALF, 128), F32)
         for x in range(nx):
-            base_high, base_low = split(inverse_ref[x * nz + z])
-            base_high = dot(order_ref[...], base_high).astype(BF16)
-            base_low = dot(order_ref[...], base_low).astype(BF16)
-            whole = dot(base_high, pair)
-            whole = whole[:, :128] + whole[:, 128:] + dot(base_low, pair[:, :128])
-            value = jnp.where(wide_part == x, whole, value)
+            high = whole[2 * HALF * x:2 * HALF * x + HALF]
+            low = whole[2 * HALF * x + HALF:2 * HALF * (x + 1)]
+            value = jnp.where(wide_part == x, high[:, :128] + high[:, 128:] + low[:, :128], value)
         start.append(value)
         current.append(value)
 
@@ -263,18 +271,24 @@
                 device_id=at(dx, dy, 0), device_id_type=MESH))
         for copy in copies:
             copy.start()
-        for copy in copies:
-            copy.wait()
-        copies = [
-            pltpu.make_async_remote_copy(
-                sites.at[sweep, :, nz - 1], below.at[sweep], send_sem.at[r, 9], got_sem.at[r, 9],
-                device_id=at(0, 0, 1), device_id_type=MESH),
-            pltpu.make_async_remote_copy(
-                sites.at[sweep], above.at[sweep], send_sem.at[r, 10], got_sem.at[r, 10],
-                device_id=at(0, 0, -1), device_id_type=MESH),
-        ]
-        for copy in copies:
-            copy.start()
+        passing = []
+        for i in range(9):
+            if i > 0:
+                slot = SLOT[(-STEPS[i][0], -STEPS[i][1])]
+                copies[i - 1].wait_recv()
+            else:
+                slot = 0
+            passing.append(pltpu.make_async_remote_copy(
+                sites.at[sweep, slot], above.at[sweep, slot],
+                pass_sem.at[0, sweep, slot], passed_sem.at[0, sweep, slot],
+                device_id=at(0, 0, -1), device_id_type=MESH))
+            passing[-1].start()
+            if cz > 2:
+                passing.append(pltpu.make_async_remote_copy(
+                    sites.at[sweep, slot, nz - 1], below.at[sweep, slot],
+                    pass_sem.at[1, sweep, slot], passed_sem.at[1, sweep, slot],
+                    device_id=at(0, 0, 1), device_id_type=MESH))
+                passing[-1].start()
 
         def gather(zs, load, sweep=sweep):
             for dy in (-1, 0, 1):
@@ -293,15 +307,17 @@
         for z in range(nz):
             gather(1 + z, lambda slot, z=z: sites[sweep, slot, z])
         for copy in copies:
+            copy.wait_send()
+        for copy in passing:
             copy.wait()
-        gather(0, lambda slot: below[sweep, slot])
+        gather(0, lambda slot: below[sweep, slot] if cz > 2 else above[sweep, slot, nz - 1])
         for z in range(2):
             gather(3 + z, lambda slot, z=z: above[sweep, slot, z])
         for z in range(nz):
             product = [jnp.zeros((2 * HALF, 256), F32) for _ in range(nx)]
             for dy in range(3):
                 right = rows[dy, :, z:z + 4].reshape(256, 256)
-                left = jnp.concatenate([operator[x * nz + z, dy] for x in range(nx)], axis=0)
+                left = operator[z, dy].reshape(2 * HALF * nx, 256)
                 whole = dot(left, right)
                 for x in range(nx):
                     product[x] = product[x] + whole[2 * HALF * x:2 * HALF * (x + 1)]
@@ -312,8 +328,11 @@
             current[z] = start[z] + (current[z] - value)
 
     for z in range(nz):
-        cells = dot(back_ref[...], joined_split(current[z]))
-        store(result_ref, z, cells[:, :128] + cells[:, 128:])
+        high, low = (lax.dot_general(v, order_ref[...], (((0,), (0,)), ((), ())),
+                                     preferred_element_type=F32) for v in split(current[z]))
+        cells = high + low
+        for x in range(nx):
+            result_ref[x * nz + z] = cells[32 * x:32 * x + 32]
 
 
 def body(sizes, displacement, dof_weight, coarse_matrix, block_inverse):
@@ -322,18 +341,22 @@
     edges = shape[3]
     rhs, dofs = shape[5], shape[6]
     coarse = block_inverse.shape[-1]
-    consts = [jnp.asarray(t) for t in tables()]
+    nx, nz = shape[0], shape[2]
+    consts = [jnp.asarray(t) for t in tables(nz)]
     vmem = pl.BlockSpec(memory_space=pltpu.VMEM)
     hbm = pl.BlockSpec(memory_space=pl.ANY)
     average, result = pl.pallas_call(
         functools.partial(kernel, sizes),
-        out_shape=[jax.ShapeDtypeStruct((cells, coarse, rhs), F32)] * 2,
+        out_shape=[
+            jax.ShapeDtypeStruct((nx, coarse * nz, rhs), F32),
+            jax.ShapeDtypeStruct((cells, rhs, coarse), F32),
+        ],
         in_specs=[hbm, vmem, hbm] + [vmem] * 7,
         out_specs=[vmem, vmem],
         scratch_shapes=[
             pltpu.VMEM((cells, 3 * edges * rhs, dofs), BF16),
-            pltpu.VMEM((27 * cells, coarse, coarse), F32),
-            pltpu.VMEM((cells, 3, 2 * HALF, 256), BF16),
+            pltpu.VMEM((27 * nx, coarse * nz, coarse), F32),
+            pltpu.VMEM((nz, 3, nx, 2 * HALF, 256), BF16),
             pltpu.VMEM((3, 3, 16, 128), F32),
             pltpu.VMEM((9, 3, 16, 128), F32),
             pltpu.VMEM((3, 2, 16, 128), F32),
@@ -342,24 +365,28 @@
             pltpu.VMEM((SWEEPS - 1, 9, 16, 128), F32),
             pltpu.VMEM((SWEEPS - 1, 9, 2, 16, 128), F32),
             pltpu.VMEM((3, 4, 5, 16, 256), BF16),
-            pltpu.VMEM((64, 128), F32),
+            pltpu.VMEM((nz, 64, 128), F32),
+            pltpu.VMEM((nz, nx, 2 * HALF, coarse), BF16),
+            pltpu.VMEM((coarse * nz, 128), F32),
             pltpu.SemaphoreType.DMA((2,)),
             pltpu.SemaphoreType.DMA((SWEEPS, 13)),
             pltpu.SemaphoreType.DMA((SWEEPS, 13)),
+            pltpu.SemaphoreType.DMA((2, SWEEPS - 1, 9)),
+            pltpu.SemaphoreType.DMA((2, SWEEPS - 1, 9)),
         ],
         compiler_params=pltpu.CompilerParams(
-            collective_id=0, has_side_effects=True, vmem_limit_bytes=40 * 1024 * 1024
+            collective_id=0, has_side_effects=True, vmem_limit_bytes=60 * 1024 * 1024
         ),
     )(
         displacement.reshape(cells, 3 * edges * rhs, dofs),
-        dof_weight.reshape(cells, edges, dofs),
-        coarse_matrix.reshape(27 * cells, coarse, coarse),
-        block_inverse.reshape(cells, coarse, coarse),
+        dof_weight.transpose(0, 1, 3, 2, 4).reshape(nx, edges * nz, dofs),
+        coarse_matrix.transpose(0, 1, 3, 4, 2, 5).reshape(27 * nx, coarse * nz, coarse),
+        block_inverse.transpose(0, 1, 3, 2, 4).reshape(nx, coarse * nz, coarse),
         *consts,
     )
     return (
-        average.reshape(shape[:3] + (edges, 3, rhs)),
-        result.reshape(shape[:3] + (coarse, rhs)),
+        average.reshape(nx, 1, edges, 3, nz, rhs).transpose(0, 1, 4, 2, 3, 5),
+        result.reshape(shape[:3] + (rhs, coarse)).transpose(0, 1, 2, 4, 3),
     )
 
 

time: 47.5 us -> 45 us (0.947)
  local copies, waits for them, and re-layouts: 6.01 us -> 3.17 us
  Pallas kernels: 40.5 us -> 41.1 us
    unnamed x19 -> x2, local copies, waits for them, and re-layouts: 5.98 us -> 3.17 us
    pallas_call x1, Pallas kernels: 40.5 us -> 41.1 us  [body(): pl.pallas_call(functools.partial(kernel, sizes), out_shape=[jax.ShapeDtyp...]
where the time goes in v2:
time: 45 us; the launch traced here: 44.9 us
  Pallas kernels  41.1 us (91%)
  local copies, waits for them, and re-layouts  3.17 us (7%)
  between operations  0.64 us (1%)
    pallas_call x1, Pallas kernels, body(): pl.pallas_call(functools.partial(kernel, sizes), out_shape=[jax.ShapeDtyp...  41.1 us
    unnamed x2, local copies, waits for them, and re-layouts  3.17 us

profile of v2, /device:TPU:0, one launch (start us, length us, event | category | flops | bytes accessed | tf_op | source)
XLA Modules:
  0.0 44.9 jit_solution(4844777739949321270)
XLA Ops:
  0.6 41.1 %shard_map.113 = (f32[4,72,32]{2,1,0:T(8,128)}, f32[8,32,36]{2,1,0:T(8,128)}) custom-call(bf16[8,1152,128]{2,1,0:T(8,128)(2,1)} %bitcast.21, bf16[4,24,128]{2,1,0:T(8,128)(2,1)} %bitcast.25, f32[108,72,36]{2,1,0:T(8,128)} %bitcast.20, f32[4,72,36]{2,1,0:T(8,128)} %bitcast.22, bf16[72,128]{1,0:T(8,128)(2,1)} %constant.12.clone.place_ref, ...), custom_call_target="tpu_custom_call" | custom-call | tf_op jit(solution)/shard_map/pallas_call | solution.py:348
  41.7 1.6 %copy.16 = f32[4,1,2,12,3,32]{5,2,4,3,1,0:T(2,128)} copy(f32[4,1,2,12,3,32]{5,2,4,3,1,0:T(2,128)} %bitcast.23) | data formatting | bytes 73728
  43.3 1.6 %copy.17 = f32[4,1,2,36,32]{3,4,2,1,0:T(8,128)} copy(f32[4,1,2,36,32]{3,4,2,1,0:T(8,128)} %bitcast.24) | data formatting | bytes 73728

commit v3 on v2

--- a/solution.py
+++ b/solution.py
@@ -19,7 +19,7 @@
     (0, 0, 0), (0, 0, 1), (1, 0, 0), (1, 0, 1),
     (0, 0, 0), (0, 1, 0), (1, 0, 0), (1, 1, 0),
 ]
-STEPS = [(0, 0)] + [s for s in itertools.product((-1, 0, 1), (-1, 0, 1)) if s != (0, 0)]
+STEPS = [(0, 0), (-1, 0), (1, 0)] + [(dx, dy) for dy, dx in itertools.product((-1, 1), (-1, 0, 1))]
 SLOT = {s: i for i, s in enumerate(STEPS)}
 HALF = 48
 PAIR = 80
@@ -77,9 +77,10 @@
     return jnp.dot(a, b, preferred_element_type=F32)
 
 
-def kernel(sizes, disp_hbm, weight_ref, matrix_hbm, inverse_ref, place_ref, spread_ref, chunk_ref,
-           fold_ref, order_ref, widen_ref, average_ref, result_ref,
-           disp, matrix, operator, main, rim, zsend, zgot, sites, below, above, rows, wide, base, cells_ref,
+def kernel(sizes, disp_hbm, weight_hbm, matrix_hbm, inverse_hbm, place_hbm, spread_hbm, chunk_hbm,
+           fold_hbm, order_hbm, widen_hbm, average_ref, result_ref,
+           weight_ref, inverse_ref, place_ref, spread_ref, chunk_ref, fold_ref, order_ref, widen_ref,
+           disp, matrix, operator, main, rim, pack, zsend, zgot, sites, below, above, rows, wide, base, cells_ref,
            load_sem, send_sem, got_sem, pass_sem, passed_sem):
     nx, nz = 4, 2
     gx, gy, gz = (lax.axis_index(a) for a in ("gx", "gy", "gz"))
@@ -90,7 +91,16 @@
 
     load_disp = pltpu.make_async_copy(disp_hbm, disp, load_sem.at[0])
     load_matrix = pltpu.make_async_copy(matrix_hbm, matrix, load_sem.at[1])
+    early = [pltpu.make_async_copy(a, b, load_sem.at[2 + i]) for i, (a, b) in enumerate(
+        ((weight_hbm, weight_ref), (spread_hbm, spread_ref), (chunk_hbm, chunk_ref)))]
+    late = [pltpu.make_async_copy(a, b, load_sem.at[5 + i]) for i, (a, b) in enumerate(
+        ((inverse_hbm, inverse_ref), (place_hbm, place_ref), (fold_hbm, fold_ref),
+         (order_hbm, order_ref), (widen_hbm, widen_ref)))]
+    for copy in early:
+        copy.start()
     load_disp.start()
+    for copy in late:
+        copy.start()
     load_matrix.start()
     barrier = pltpu.get_barrier_semaphore()
     for dx, dy in STEPS[1:]:
@@ -103,7 +113,11 @@
     part = lane // 32
     ones = jnp.ones((128, 128), BF16)
     zero = jnp.zeros((16, 128), F32)
-
+    few = row[:8] < 3
+    next_few = (row[:8] >= 3) & (row[:8] < 6)
+
+    for copy in early:
+        copy.wait()
     load_disp.wait()
     number = {}
     mass = {}
@@ -136,7 +150,12 @@
                     heavy = mass[x * nz + z][b:b + 16]
                     edge = edge + jnp.where(lane // 8 == 4 + x + ox, heavy, 0.0)
         main[1, zs] = body
-        rim[0, zs] = edge + jnp.where(part == 3, pltpu.roll(body, 96, 1), 0.0)
+        edge = edge + jnp.where(part == 3, pltpu.roll(body, 96, 1), 0.0)
+        rim[0, zs] = edge
+        for k, value in enumerate((body, edge)):
+            first, second = value[:8], value[8:]
+            pack[0, k, zs] = jnp.where(few, first, pltpu.roll(second, 3, 0))
+            pack[1, k, zs] = jnp.where(few, pltpu.roll(first, 5, 0), second)
 
     pl.semaphore_wait(barrier, 10)
     copies = []
@@ -144,17 +163,22 @@
         if i == 0:
             continue
         slot = SLOT[(-dx, -dy)]
+        packed = (dy + 1) // 2
         copies.append(pltpu.make_async_remote_copy(
-            rim.at[0], rim.at[slot], send_sem.at[0, i], got_sem.at[0, slot],
+            pack.at[packed, 1] if dy else rim.at[0],
+            rim.at[slot, :, pl.ds(0, 8)] if dy else rim.at[slot],
+            send_sem.at[0, i], got_sem.at[0, slot],
             device_id=at(dx, dy, 0), device_id_type=MESH))
-        if dx == 0:
+        if dx == 0 and dy:
             copies.append(pltpu.make_async_remote_copy(
-                main.at[1], main.at[1 - dy], send_sem.at[0, 11 + (dy + 1) // 2],
-                got_sem.at[0, 11 + (1 - dy) // 2],
+                pack.at[packed, 0], main.at[1 - dy, :, pl.ds(0, 8)], send_sem.at[0, 11 + packed],
+                got_sem.at[0, 12 - packed],
                 device_id=at(dx, dy, 0), device_id_type=MESH))
     for copy in copies:
         copy.start()
 
+    for copy in late:
+        copy.wait()
     load_matrix.wait()
 
     def prepare(x, carry):
@@ -188,22 +212,24 @@
     for copy in copies:
         copy.wait()
 
-    lower = (row % 8) < 3
-    upper = ((row % 8) >= 3) & ((row % 8) < 6)
     for zs in range(nz + 1):
         sums = {}
         for dy in (-1, 0, 1):
-            before = rim[SLOT[(-1, dy)], zs]
-            after = pltpu.roll(rim[SLOT[(1, dy)], zs], 32, 1)
-            body = main[1 + dy, zs] + jnp.where(part == 0, before, 0.0)
-            edge = (rim[SLOT[(0, dy)], zs]
-                    + jnp.where(lane // 8 == 4, pltpu.roll(before, 96, 1), 0.0)
-                    + jnp.where((part == 0) | (lane // 8 == 8), after, 0.0))
+            count = 8 if dy else 16
+            spot, eighth = part[:count], lane[:count] // 8
+            before = rim[SLOT[(-1, dy)], zs, :count]
+            after = pltpu.roll(rim[SLOT[(1, dy)], zs, :count], 32, 1)
+            body = main[1 + dy, zs, :count] + jnp.where(spot == 0, before, 0.0)
+            edge = (rim[SLOT[(0, dy)], zs, :count]
+                    + jnp.where(eighth == 4, pltpu.roll(before, 96, 1), 0.0)
+                    + jnp.where((spot == 0) | (eighth == 8), after, 0.0))
             sums[dy] = (body, edge)
         for k in range(2):
-            zsend[zs, k] = (sums[0][k]
-                            + jnp.where(lower, pltpu.roll(sums[-1][k], 13, 0), 0.0)
-                            + jnp.where(upper, pltpu.roll(sums[1][k], 3, 0), 0.0))
+            low, high = sums[-1][k], sums[1][k]
+            zsend[zs, k] = sums[0][k] + jnp.concatenate([
+                jnp.where(few, low, jnp.where(next_few, pltpu.roll(high, 3, 0), 0.0)),
+                jnp.where(few, pltpu.roll(low, 5, 0), jnp.where(next_few, high, 0.0)),
+            ], axis=0)
     copies = [
         pltpu.make_async_remote_copy(zsend.at[nz], zgot.at[0], send_sem.at[0, 9], got_sem.at[0, 9],
                                      device_id=at(0, 0, 1), device_id_type=MESH),
@@ -261,66 +287,74 @@
         r = sweep + 1
         for z in range(nz):
             sites[sweep, 0, z] = current[z][:16]
-        copies = []
-        for i, (dx, dy) in enumerate(STEPS):
-            if i == 0:
-                continue
+        coming = {}
+        for i in (*range(3, 9), 1, 2):
+            dx, dy = STEPS[i]
             slot = SLOT[(-dx, -dy)]
-            copies.append(pltpu.make_async_remote_copy(
+            coming[slot] = pltpu.make_async_remote_copy(
                 sites.at[sweep, 0], sites.at[sweep, slot], send_sem.at[r, i], got_sem.at[r, slot],
-                device_id=at(dx, dy, 0), device_id_type=MESH))
-        for copy in copies:
-            copy.start()
-        passing = []
-        for i in range(9):
-            if i > 0:
-                slot = SLOT[(-STEPS[i][0], -STEPS[i][1])]
-                copies[i - 1].wait_recv()
-            else:
-                slot = 0
-            passing.append(pltpu.make_async_remote_copy(
+                device_id=at(dx, dy, 0), device_id_type=MESH)
+            coming[slot].start()
+        passing = {}
+
+        def forward(slot):
+            if slot > 0:
+                coming[slot].wait_recv()
+            passing[slot] = [pltpu.make_async_remote_copy(
                 sites.at[sweep, slot], above.at[sweep, slot],
                 pass_sem.at[0, sweep, slot], passed_sem.at[0, sweep, slot],
-                device_id=at(0, 0, -1), device_id_type=MESH))
-            passing[-1].start()
+                device_id=at(0, 0, -1), device_id_type=MESH)]
             if cz > 2:
-                passing.append(pltpu.make_async_remote_copy(
+                passing[slot].append(pltpu.make_async_remote_copy(
                     sites.at[sweep, slot, nz - 1], below.at[sweep, slot],
                     pass_sem.at[1, sweep, slot], passed_sem.at[1, sweep, slot],
                     device_id=at(0, 0, 1), device_id_type=MESH))
-                passing[-1].start()
-
-        def gather(zs, load, sweep=sweep):
-            for dy in (-1, 0, 1):
-                own, before, after = (load(SLOT[(s, dy)]) for s in (0, -1, 1))
-                shifted = [
-                    jnp.where(part == 0, pltpu.roll(before, 32, 1), pltpu.roll(own, 32, 1)),
-                    own,
-                    jnp.where(part == 3, pltpu.roll(after, 96, 1), pltpu.roll(own, 96, 1)),
-                    jnp.where(part >= 2, pltpu.roll(after, 64, 1), pltpu.roll(own, 64, 1)),
-                ]
-                for s in range(4):
-                    high, low = split(shifted[s])
-                    rows[dy + 1, s, zs, :, :128] = high
-                    rows[dy + 1, s, zs, :, 128:] = low
-
+            for copy in passing[slot]:
+                copy.start()
+
+        def gather(dy, zs, load):
+            own, before, after = (load(SLOT[(s, dy)]) for s in (0, -1, 1))
+            shifted = [
+                jnp.where(part == 0, pltpu.roll(before, 32, 1), pltpu.roll(own, 32, 1)),
+                own,
+                jnp.where(part == 3, pltpu.roll(after, 96, 1), pltpu.roll(own, 96, 1)),
+                jnp.where(part >= 2, pltpu.roll(after, 64, 1), pltpu.roll(own, 64, 1)),
+            ]
+            for s in range(4):
+                high, low = split(shifted[s])
+                rows[dy + 1, s, zs, :, :128] = high
+                rows[dy + 1, s, zs, :, 128:] = low
+
+        def gather_all(dy):
+            for z in range(nz):
+                gather(dy, 1 + z, lambda slot: sites[sweep, slot, z])
+            for s in (0, -1, 1):
+                for copy in passing[SLOT[(s, dy)]]:
+                    copy.wait_recv()
+            gather(dy, 0, lambda slot: below[sweep, slot] if cz > 2 else above[sweep, slot, nz - 1])
+            for z in range(2):
+                gather(dy, 3 + z, lambda slot: above[sweep, slot, z])
+
+        def multiply(z, dy):
+            left = operator[z, dy + 1].reshape(2 * HALF * nx, 256)
+            return dot(left, rows[dy + 1, :, z:z + 4].reshape(256, 256))
+
+        for slot in range(3):
+            forward(slot)
+        gather_all(0)
+        products = [multiply(z, 0) for z in range(nz)]
+        for slot in range(3, 9):
+            forward(slot)
+        for dy in (-1, 1):
+            gather_all(dy)
+            products = [products[z] + multiply(z, dy) for z in range(nz)]
+        for slot in range(9):
+            if slot > 0:
+                coming[slot].wait_send()
+            for copy in passing[slot]:
+                copy.wait_send()
         for z in range(nz):
-            gather(1 + z, lambda slot, z=z: sites[sweep, slot, z])
-        for copy in copies:
-            copy.wait_send()
-        for copy in passing:
-            copy.wait()
-        gather(0, lambda slot: below[sweep, slot] if cz > 2 else above[sweep, slot, nz - 1])
-        for z in range(2):
-            gather(3 + z, lambda slot, z=z: above[sweep, slot, z])
-        for z in range(nz):
-            product = [jnp.zeros((2 * HALF, 256), F32) for _ in range(nx)]
-            for dy in range(3):
-                right = rows[dy, :, z:z + 4].reshape(256, 256)
-                left = operator[z, dy].reshape(2 * HALF * nx, 256)
-                whole = dot(left, right)
-                for x in range(nx):
-                    product[x] = product[x] + whole[2 * HALF * x:2 * HALF * (x + 1)]
+            product = [products[z][2 * HALF * x:2 * HALF * (x + 1)] for x in range(nx)]
             value = jnp.zeros((HALF, 128), F32)
             for x in range(nx):
                 whole = product[x][:HALF, :128] + product[x][:HALF, 128:] + product[x][HALF:, :128]
@@ -351,14 +385,18 @@
             jax.ShapeDtypeStruct((nx, coarse * nz, rhs), F32),
             jax.ShapeDtypeStruct((cells, rhs, coarse), F32),
         ],
-        in_specs=[hbm, vmem, hbm] + [vmem] * 7,
+        in_specs=[hbm] * 10,
         out_specs=[vmem, vmem],
         scratch_shapes=[
+            pltpu.VMEM((nx, edges * nz, dofs), BF16),
+            pltpu.VMEM((nx, coarse * nz, coarse), F32),
+            *[pltpu.VMEM(t.shape, t.dtype) for t in consts],
             pltpu.VMEM((cells, 3 * edges * rhs, dofs), BF16),
             pltpu.VMEM((27 * nx, coarse * nz, coarse), F32),
             pltpu.VMEM((nz, 3, nx, 2 * HALF, 256), BF16),
             pltpu.VMEM((3, 3, 16, 128), F32),
             pltpu.VMEM((9, 3, 16, 128), F32),
+            pltpu.VMEM((2, 2, 3, 8, 128), F32),
             pltpu.VMEM((3, 2, 16, 128), F32),
             pltpu.VMEM((2, 2, 16, 128), F32),
             pltpu.VMEM((SWEEPS - 1, 9, 2, 16, 128), F32),
@@ -368,7 +406,7 @@
             pltpu.VMEM((nz, 64, 128), F32),
             pltpu.VMEM((nz, nx, 2 * HALF, coarse), BF16),
             pltpu.VMEM((coarse * nz, 128), F32),
-            pltpu.SemaphoreType.DMA((2,)),
+            pltpu.SemaphoreType.DMA((10,)),
             pltpu.SemaphoreType.DMA((SWEEPS, 13)),
             pltpu.SemaphoreType.DMA((SWEEPS, 13)),
             pltpu.SemaphoreType.DMA((2, SWEEPS - 1, 9)),

time: 45 us -> 41.7 us (0.927)
  Pallas kernels: 41.1 us -> 37.7 us
    pallas_call x1, Pallas kernels: 41.1 us -> 37.7 us  [body(): pl.pallas_call(functools.partial(kernel, sizes), out_shape=[jax.ShapeDtyp...]
where the time goes in v3:
time: 41.7 us; the launch traced here: 41.5 us
  Pallas kernels  37.7 us (90%)
  local copies, waits for them, and re-layouts  3.17 us (8%)
  between operations  0.64 us (2%)
    pallas_call x1, Pallas kernels, body(): pl.pallas_call(functools.partial(kernel, sizes), out_shape=[jax.ShapeDtyp...  37.7 us
    unnamed x2, local copies, waits for them, and re-layouts  3.17 us

profile of v3, /device:TPU:0, one launch (start us, length us, event | category | flops | bytes accessed | tf_op | source)
XLA Modules:
  0.0 41.5 jit_solution(1075697706355435910)
XLA Ops:
  0.6 37.7 %shard_map.113 = (f32[4,72,32]{2,1,0:T(8,128)}, f32[8,32,36]{2,1,0:T(8,128)}) custom-call(bf16[8,1152,128]{2,1,0:T(8,128)(2,1)} %bitcast.21, bf16[4,24,128]{2,1,0:T(8,128)(2,1)} %bitcast.25, f32[108,72,36]{2,1,0:T(8,128)} %bitcast.20, f32[4,72,36]{2,1,0:T(8,128)} %bitcast.22, bf16[72,128]{1,0:T(8,128)(2,1)} %constant.12.clone.place_hbm, ...), custom_call_target="tpu_custom_call" | custom-call | tf_op jit(solution)/shard_map/pallas_call | solution.py:382
  38.3 1.6 %copy.16 = f32[4,1,2,12,3,32]{5,2,4,3,1,0:T(2,128)} copy(f32[4,1,2,12,3,32]{5,2,4,3,1,0:T(2,128)} %bitcast.23) | data formatting | bytes 73728
  39.9 1.6 %copy.17 = f32[4,1,2,36,32]{3,4,2,1,0:T(8,128)} copy(f32[4,1,2,36,32]{3,4,2,1,0:T(8,128)} %bitcast.24) | data formatting | bytes 73728
